TPU v7x, 256 devices: a whole 4x4x8 slice. The times are simulated.
256 devices in a mesh: head: 4 (over y_lo, core), inner: 16 (over y_hi, z), outer: 4 (over x).
Axes of the slice: x: 4, y: 4 (y_hi: 2, y_lo: 2; y = y_hi * 2 + y_lo), z: 8, core: 2. Of those that a mesh axis runs over, the one named last changes fastest.
Arguments:
- queries: bfloat16 [8192, 3072], P(('head', 'inner', 'outer')), may hold values from -8 to 8
- keys: bfloat16 [8192, 512], P(('head', 'inner', 'outer')), may hold values from -6 to 6
- values: bfloat16 [8192, 512], P(('head', 'inner', 'outer')), may hold values from -6 to 6
- outputs: bfloat16 [8192, 3072], P(('head', 'inner', 'outer')), may hold values from -6 to 6
- log_norms: bfloat16 [8192, 24], P(('head', 'inner', 'outer')), as said below
- grad_output: bfloat16 [8192, 6144], P(('head', 'inner', 'outer')), may hold values from -6 to 6
- w_output: bfloat16 [3072, 6144], P('head', 'inner'), may hold values from -0.078125 to 0.078125
- block_order: int32 [256], replicated, may hold values from 0 to 255, as said below
Outputs:
- grad_query: bfloat16 [8192, 3072], P(('head', 'inner', 'outer'))
- grad_key: bfloat16 [8192, 512], P(('head', 'inner', 'outer'))
- grad_value: bfloat16 [8192, 512], P(('head', 'inner', 'outer'))
Inputs may be any that keep to these rules, and one draw needn't show every extreme that they name: `block_order`: a permutation of the 256 sequence blocks. `log_norms`: drawn as log(p + 1) + 1.1 + 0.5 u, where p is the row's sequence position and u is uniform in [0, 1); it stands in for a stored log-sum-exp and is not recomputed from queries and keys.
All inputs are finite; a program needn't handle non-finite values.
Results may differ from a plain program's by a relative error of at most 0.018.
Values may be sent and summed in bfloat16 or wider, within the bound.
No kernel may reach another device: no remote copies, remote signals or barrier semaphores. Data moves between devices by JAX's collectives and lax.ppermute only.
A program may use at most 128 MiB of HBM per device.

v0:
```python
import jax
import jax.numpy as jnp
from jax import lax
from jax.sharding import PartitionSpec as P

HD = 128


def from_behind(block, axis, distance):
    devices = range(lax.axis_size(axis))
    route = [((i - distance) % len(devices), i) for i in devices]
    return lax.ppermute(block, axis, route)


def tile_terms(
    query_part, dattn_part, norm_part, delta_part, key_part, value_part, row_pos, col_pos
):
    row_count = query_part.shape[0]
    col_count = key_part.shape[0]
    kv_heads = key_part.shape[1] // HD
    group_size = query_part.shape[1] // key_part.shape[1]
    score_scale = HD ** (-0.5)
    query_four = query_part.reshape(row_count, kv_heads, group_size, HD)
    dattn_four = dattn_part.reshape(row_count, kv_heads, group_size, HD)
    key_three = key_part.reshape(col_count, kv_heads, HD)
    value_three = value_part.reshape(col_count, kv_heads, HD)
    scores = (
        jnp.einsum("qgjd,kgd->gjqk", query_four, key_three, preferred_element_type=jnp.float32)
        * score_scale
    )
    norm_four = (
        norm_part.astype(jnp.float32)
        .reshape(row_count, kv_heads, group_size)
        .transpose(1, 2, 0)[..., None]
    )
    visible = row_pos[:, None] >= col_pos[None, :]
    probs = jnp.where(visible, jnp.exp(scores - norm_four), jnp.float32(0.0))
    probs_low = probs.astype(jnp.bfloat16)
    grad_v = jnp.einsum("gjqk,qgjd->kgd", probs_low, dattn_four, preferred_element_type=jnp.float32)
    grad_probs = jnp.einsum(
        "qgjd,kgd->gjqk", dattn_four, value_three, preferred_element_type=jnp.float32
    )
    centre = delta_part.reshape(row_count, kv_heads, group_size).transpose(1, 2, 0)[..., None]
    grad_scores = (probs * (grad_probs - centre)).astype(jnp.bfloat16)
    grad_q = (
        jnp.einsum("gjqk,kgd->qgjd", grad_scores, key_three, preferred_element_type=jnp.float32)
        * score_scale
    )
    grad_k = (
        jnp.einsum("gjqk,qgjd->kgd", grad_scores, query_four, preferred_element_type=jnp.float32)
        * score_scale
    )
    return (
        grad_q.reshape(row_count, -1),
        grad_k.reshape(col_count, -1),
        grad_v.reshape(col_count, -1),
    )


def body(queries, keys, values, outputs, log_norms, grad_output, w_output, block_order):
    tok_rows = grad_output.shape[0]
    inner_count = lax.axis_size("inner")
    outer_count = lax.axis_size("outer")
    ctx_count = inner_count * outer_count
    inner_index = lax.axis_index("inner")
    outer_index = lax.axis_index("outer")
    my_rank = inner_index * outer_count + outer_index
    grad_rows = lax.all_gather(grad_output, "head", axis=0, tiled=True)
    query_width = w_output.shape[0]
    grad_attn = lax.dot_general(
        grad_rows,
        lax.all_gather(w_output, "inner", axis=1, tiled=True),
        (((1,), (1,)), ((), ())),
        preferred_element_type=jnp.float32,
    ).astype(jnp.bfloat16)
    query_local, key_local, value_local, output_local, norm_local = (
        lax.all_to_all(queries, "head", split_axis=1, concat_axis=0, tiled=True),
        lax.all_to_all(keys, "head", split_axis=1, concat_axis=0, tiled=True),
        lax.all_to_all(values, "head", split_axis=1, concat_axis=0, tiled=True),
        lax.all_to_all(outputs, "head", split_axis=1, concat_axis=0, tiled=True),
        lax.all_to_all(log_norms, "head", split_axis=1, concat_axis=0, tiled=True),
    )
    row_count = query_local.shape[0]
    key_width = key_local.shape[1]
    delta = jnp.sum(
        (grad_attn.astype(jnp.float32) * output_local.astype(jnp.float32)).reshape(
            row_count, -1, HD
        ),
        axis=2,
    )
    sub_count = row_count // tok_rows
    offsets = jnp.arange(tok_rows, dtype=jnp.int32)

    def positions(owner_rank):
        block_ids = block_order[jnp.arange(sub_count, dtype=jnp.int32) * ctx_count + owner_rank]
        return (block_ids, (block_ids[:, None] * tok_rows + offsets[None, :]).reshape(-1))

    my_ids, my_pos = positions(my_rank)

    def step_terms(key_now, value_now, owner_rank):
        their_ids, their_pos = positions(owner_rank)
        return tile_terms(
            query_local, grad_attn, norm_local, delta, key_now, value_now, my_pos, their_pos
        )

    query_total = jnp.zeros((row_count, query_width), jnp.float32)
    grad_state = jnp.zeros((ctx_count * row_count, 2 * key_width), jnp.float32)
    key_now = key_local
    value_now = value_local
    for lap_index in range(outer_count):
        source_outer = (outer_index - lap_index) % outer_count

        def inner_step(step_index, carry):
            key_cur, value_cur, query_acc, state_cur = carry
            owner_rank = (inner_index - step_index) % inner_count * outer_count + source_outer
            part_q, part_k, part_v = step_terms(key_cur, value_cur, owner_rank)
            key_cur, value_cur = from_behind((key_cur, value_cur), "inner", 1)
            state_cur = lax.dynamic_update_slice_in_dim(
                state_cur, jnp.concatenate([part_k, part_v], 1), owner_rank * row_count, 0
            )
            return (key_cur, value_cur, query_acc + part_q, state_cur)

        key_now, value_now, query_total, grad_state = lax.fori_loop(
            0, inner_count, inner_step, (key_now, value_now, query_total, grad_state)
        )
        if lap_index + 1 < outer_count:
            key_now, value_now = from_behind((key_now, value_now), "outer", 1)
    summed = lax.psum_scatter(grad_state, ("inner", "outer"), scatter_dimension=0, tiled=True)
    key_total = summed[:, :key_width]
    value_total = summed[:, key_width:]
    grad_query, grad_key, grad_value = (
        lax.all_to_all(
            query_total.astype(jnp.bfloat16), "head", split_axis=0, concat_axis=1, tiled=True
        ),
        lax.all_to_all(
            key_total.astype(jnp.bfloat16), "head", split_axis=0, concat_axis=1, tiled=True
        ),
        lax.all_to_all(
            value_total.astype(jnp.bfloat16), "head", split_axis=0, concat_axis=1, tiled=True
        ),
    )
    return (grad_query, grad_key, grad_value)


def solution(mesh):
    in_specs = (
        P(("head", "inner", "outer"), None),
        P(("head", "inner", "outer"), None),
        P(("head", "inner", "outer"), None),
        P(("head", "inner", "outer"), None),
        P(("head", "inner", "outer"), None),
        P(("head", "inner", "outer"), None),
        P("head", "inner"),
        P(),
    )
    out_specs = (
        P(("head", "inner", "outer"), None),
        P(("head", "inner", "outer"), None),
        P(("head", "inner", "outer"), None),
    )
    return jax.shard_map(body, mesh=mesh, in_specs=in_specs, out_specs=out_specs, check_vma=False)
```

profile of v0, /device:TPU:1, one launch (start us, length us, event | category | flops | bytes accessed | tf_op | source)
XLA Modules:
  0.0 1151.4 jit_solution(15804857690926209388)
XLA Ops:
  10.0 6.5 all-to-all-start.3
  19.5 3.9 all-to-all-start
  28.0 3.4 all-to-all-start.2
  32.8 5.6 all-to-all-done.2
  38.4 4.2 all-to-all-start.4
  42.9 4.1 all-to-all-done.4
  47.0 4.1 all-to-all-start.1
  51.1 152.3 %all-gather.5.cloned.1.call-done = bf16[768,6144]{1,0:T(8,128)(2,1)} async-done(((bf16[768,384]{1,0:T(8,128)(2,1)}), bf16[768,6144]{1,0:T(8,128)(2,1)}) %all-gather.5.cloned.1.call-update) | async-done | bytes 9437200 | tf_op jit(solution)/shard_map/all_gather | solution.py:72
  203.5 7.4 bitcast_multiply_fusion
  211.3 4.2 broadcast_in_dim.152
  215.5 109.1 %while.91 = (s32[]{:T(128)}, bf16[128,128]{0,1:T(8,128)(2,1)S(1)}, bf16[128,128]{1,0:T(8,128)(2,1)S(1)}, f32[128,768]{0,1:T(8,128)S(1)}, f32[8192,256]{0,1:T(8,1...) while((s32[]{:T(128)}, bf16[128,128]{0,1:T(8,128)(2,1)S(1)}, ...), condition=%wide.region_2.3_spmd.clone, body=%wide.region_1.2_spmd.clone.sunk | while | flops 126879784 | bytes 5065830 | solution.py:123
  239.2 3.8 collective-permute-done.6
  286.6 3.9 collective-permute-done.6
  330.0 109.5 %while.88 = (s32[]{:T(128)}, bf16[128,128]{0,1:T(8,128)(2,1)S(1)}, bf16[128,128]{1,0:T(8,128)(2,1)S(1)}, f32[128,768]{0,1:T(8,128)S(1)}, f32[8192,256]{0,1:T(8,1...) while((s32[]{:T(128)}, bf16[128,128]{0,1:T(8,128)(2,1)S(1)}, ...), condition=%wide.region_4.5_spmd.clone, body=%wide.region_3.4_spmd.clone.sunk | while | flops 126781480 | bytes 5065820 | solution.py:123
  333.1 3.3 collective-permute-done
  346.6 3.3 collective-permute-done
  360.1 3.3 collective-permute-done
  366.8 3.3 collective-permute-done
  380.3 3.9 collective-permute-done
  394.7 3.3 collective-permute-done
  414.9 3.3 collective-permute-done
  421.6 3.3 collective-permute-done
  428.4 3.9 collective-permute-done
  435.9 3.3 collective-permute-done
  443.8 109.2 %while.89 = (s32[]{:T(128)}, bf16[128,128]{0,1:T(8,128)(2,1)S(1)}, bf16[128,128]{1,0:T(8,128)(2,1)S(1)}, f32[128,768]{0,1:T(8,128)S(1)}, f32[8192,256]{0,1:T(8,1...) while((s32[]{:T(128)}, bf16[128,128]{0,1:T(8,128)(2,1)S(1)}, ...), condition=%wide.region_6.7_spmd.clone, body=%wide.region_5.6_spmd.clone.sunk | while | flops 126781480 | bytes 5065820 | solution.py:123
  446.9 3.3 collective-permute-done.2
  453.7 3.3 collective-permute-done.2
  460.4 3.9 collective-permute-done.2
  468.1 3.3 collective-permute-done.2
  501.8 3.3 collective-permute-done.2
  515.2 3.3 collective-permute-done.2
  522.0 3.9 collective-permute-done.2
  529.2 3.3 collective-permute-done.2
  535.9 3.3 collective-permute-done.2
  549.4 3.3 collective-permute-done.2
  553.1 4.3 collective-permute-done.12
  557.7 109.0 %while.90 = (s32[]{:T(128)}, bf16[128,128]{0,1:T(8,128)(2,1)S(1)}, bf16[128,128]{1,0:T(8,128)(2,1)S(1)}, f32[128,768]{0,1:T(8,128)S(1)}, f32[8192,256]{0,1:T(8,1...) while((s32[]{:T(128)}, bf16[128,128]{0,1:T(8,128)(2,1)S(1)}, ...), condition=%wide.region_8.9_spmd.clone, body=%wide.region_7.8_spmd.clone.sunk | while | flops 126781480 | bytes 5065820 | solution.py:123
  560.7 3.3 collective-permute-done.4
  587.7 3.3 collective-permute-done.4
  601.2 3.9 collective-permute-done.4
  608.6 3.3 collective-permute-done.4
  642.3 3.3 collective-permute-done.4
  662.5 3.9 collective-permute-done.4
  666.6 9.1 copy.170
  676.6 82.6 %all-to-all-start.5 = ((bf16[4,32,768]{2,1,0:T(8,128)(2,1)}), bf16[4,32,768]{2,1,0:T(8,128)(2,1)S(1)}, u32[]{:S(2)}, u32[]{:S(2)}) async-start(bf16[4,32,768]{2,1,0:T(8,128)(2,1)} %bitcast.12), calls=%async_computation.5 | async-start | bytes 393216 | tf_op jit(solution)/shard_map/all_to_all | solution.py:132
  759.1 323.8 %reduce-scatter.2.cloned.1.call-done = f32[128,256]{1,0:T(8,128)} async-done(((f32[8192,256]{1,0:T(8,128)}), f32[128,256]{1,0:T(8,128)}) %reduce-scatter.2.cloned.1.call-update) | async-done | bytes 131088 | tf_op jit(solution)/shard_map/reduce_scatter | solution.py:128
  1084.5 49.4 %all-to-all-start.7 = ((bf16[4,32,128]{2,1,0:T(8,128)(2,1)}), bf16[4,32,128]{2,1,0:T(8,128)(2,1)S(1)}, u32[]{:S(2)}, u32[]{:S(2)}) async-start(bf16[4,32,128]{2,1,0:T(8,128)(2,1)} %bitcast.16), calls=%async_computation.8 | async-start | bytes 65536 | tf_op jit(solution)/shard_map/all_to_all | solution.py:138
  1137.1 4.0 all-to-all-start.6
  (1495 shorter events, 364.2 us)
Async XLA Ops:
  7.2 44.0 %all-gather.3.cloned.1.call-start = ((), (), s32[]{:S(2)}) async-start(), calls=%async_computation.9 | async-start | bytes 1966080 | tf_op jit(solution)/shard_map/all_gather | solution.py:68
  7.9 195.5 %all-gather.5.cloned.1.call-start = ((), (), s32[]{:S(2)}) async-start(), calls=%async_computation.10 | async-start | bytes 10027008 | tf_op jit(solution)/shard_map/all_gather | solution.py:72
  10.0 9.6 all-to-all-start.3
  19.5 8.5 all-to-all-start
  28.0 10.3 all-to-all-start.2
  38.4 8.6 all-to-all-start.4
  47.0 164.2 %all-to-all-start.1 = ((bf16[32,4,128]{2,0,1:T(8,128)(2,1)}), bf16[32,4,128]{2,0,1:T(8,128)(2,1)S(1)}, u32[]{:S(2)}, u32[]{:S(2)}) async-start(bf16[32,4,128]{2,0,1:T(8,128)(2,1)} %copy_bitcast_fusion.4), calls=%async_computation.1 | async-start | bytes 65536 | tf_op jit(solution)/shard_map/all_to_all | solution.py:79
  51.1 1031.8 %reduce-scatter.2.cloned.1.call-start = ((), (), s32[]{:S(2)}) async-start(), calls=%async_computation.11 | async-start | bytes 8519680 | tf_op jit(solution)/shard_map/reduce_scatter | solution.py:128
  222.6 6.7 collective-permute-start.7
  229.4 6.7 collective-permute-start.7
  236.1 6.9 collective-permute-start.6
  236.1 7.0 collective-permute-start.7
  243.1 6.7 collective-permute-start.7
  249.9 6.7 collective-permute-start.7
  256.6 6.7 collective-permute-start.7
  263.3 6.7 collective-permute-start.7
  270.1 6.7 collective-permute-start.7
  276.8 6.7 collective-permute-start.7
  283.5 7.0 collective-permute-start.6
  283.5 7.4 collective-permute-start.7
  290.9 6.7 collective-permute-start.7
  297.7 6.7 collective-permute-start.7
  304.4 6.7 collective-permute-start.7
  311.1 6.7 collective-permute-start.7
  317.9 6.7 collective-permute-start.7
  336.8 6.7 collective-permute-start.1
  343.5 6.7 collective-permute-start.1
  350.2 6.7 collective-permute-start.1
  357.0 6.7 collective-permute-start.1
  363.7 6.7 collective-permute-start.1
  370.4 6.7 collective-permute-start.1
  377.2 7.0 collective-permute-start
  377.2 7.7 collective-permute-start.1
  384.9 6.7 collective-permute-start.1
  391.6 6.7 collective-permute-start.1
  425.3 7.0 collective-permute-start
  425.3 7.5 collective-permute-start.1
  457.3 7.0 collective-permute-start.2
  457.3 7.7 collective-permute-start.3
  518.9 7.0 collective-permute-start.2
  518.9 7.2 collective-permute-start.3
  598.1 7.0 collective-permute-start.4
  598.1 7.4 collective-permute-start.5
  659.4 7.0 collective-permute-start.4
  659.4 7.2 collective-permute-start.5
  676.6 407.9 %all-to-all-start.5 = ((bf16[4,32,768]{2,1,0:T(8,128)(2,1)}), bf16[4,32,768]{2,1,0:T(8,128)(2,1)S(1)}, u32[]{:S(2)}, u32[]{:S(2)}) async-start(bf16[4,32,768]{2,1,0:T(8,128)(2,1)} %bitcast.12), calls=%async_computation.5 | async-start | bytes 393216 | tf_op jit(solution)/shard_map/all_to_all | solution.py:132
  1084.5 52.6 %all-to-all-start.7 = ((bf16[4,32,128]{2,1,0:T(8,128)(2,1)}), bf16[4,32,128]{2,1,0:T(8,128)(2,1)S(1)}, u32[]{:S(2)}, u32[]{:S(2)}) async-start(bf16[4,32,128]{2,1,0:T(8,128)(2,1)} %bitcast.16), calls=%async_computation.8 | async-start | bytes 65536 | tf_op jit(solution)/shard_map/all_to_all | solution.py:138
  1137.1 7.2 all-to-all-start.6
  (99 other events, 791.4 us)
Sparse Core Ops, SparseCore 0:
  9.8 33.6 all-gather.2
  46.0 157.3 all-gather.4
  675.9 407.0 reduce-scatter.1
where the time goes:
time: 1150 us
  waiting for transfers between devices  742 us (65%)
  starting transfers between devices  168 us (15%)
  local copies, waits for them, and re-layouts  77.6 us (7%)
  matrix products  76.8 us (7%)
  other arithmetic  65.2 us (6%)
  between operations  13.8 us (1%)
    reduce_scatter x1, waiting for transfers between devices, body(): lax.psum_scatter(grad_state, ('inner', 'outer'), scatter_dimension=0, til...  324 us
    ppermute x134, waiting for transfers between devices, from_behind(): return lax.ppermute(block, axis, route)  247 us
    all_gather x1, waiting for transfers between devices, body(): lax.all_gather(w_output, 'inner', axis=1, tiled=True)  152 us
    all_to_all x1, starting transfers between devices, body(): lax.all_to_all(query_total.astype(jnp.bfloat16), 'head', split_axis=0, co...  82.6 us
    all_to_all x1, starting transfers between devices, body(): lax.all_to_all(value_total.astype(jnp.bfloat16), 'head', split_axis=0, co...  49.4 us
    dynamic_update_slice x64, other arithmetic, inner_step(): lax.dynamic_update_slice_in_dim(state_cur, jnp.concatenate([part_k, part_...  44 us
    gather x65, local copies, waits for them, and re-layouts, positions(): block_order[jnp.arange(sub_count, dtype=jnp.int32) * ctx_count + owner_rank]  42.3 us
  transfers between devices with their start and end apart: 145, of which 141 were waited for; matrix products, arithmetic and copies ran while one was open for 18% of the time, Pallas kernels for 0%

commit v1 on v0

v1 whole, which is shorter than its diff:
```python
import jax
import jax.numpy as jnp
from jax import lax
from jax.experimental import pallas as pl
from jax.experimental.pallas import tpu as pltpu
from jax.sharding import PartitionSpec as P

HD = 128
LANES = 128
BF = jnp.bfloat16
F32 = jnp.float32
HIDE = -1e30
SCALE = HD ** (-0.5)
LOG2E = 1.4426950408889634
ID_LANE = 32
CHUNK = 256
VMEM_BYTES = 48 * 1024 * 1024


def call(kernel, out_shape, **options):
    return pl.pallas_call(
        kernel,
        out_shape=out_shape,
        compiler_params=pltpu.CompilerParams(vmem_limit_bytes=VMEM_BYTES),
        **options,
    )


def xor_route(axis, mask):
    return [(i, i ^ mask) for i in range(lax.axis_size(axis))]


def split_three(x):
    high = x.astype(BF)
    rest = x - high.astype(F32)
    mid = rest.astype(BF)
    low = (rest - mid.astype(F32)).astype(BF)
    return high, mid, low


def pick_three(x, lane_rest):
    high, mid, low = split_three(x)
    zero = jnp.zeros_like(x)
    return (
        jnp.where(lane_rest == 0, high.astype(F32), zero)
        + jnp.where(lane_rest == 1, mid.astype(F32), zero)
        + jnp.where(lane_rest == 2, low.astype(F32), zero)
    ).astype(BF)


def lane_head(shape):
    lane = lax.broadcasted_iota(jnp.int32, shape, len(shape) - 1)
    head = lax.shift_right_logical(lane * 171, 9)
    return lane, head, lane - 3 * head


def pack_tokens_kernel(q_ref, o_ref, k_ref, v_ref, n_ref, out_ref):
    head_groups, rows, _ = out_ref.shape
    group = n_ref.shape[1] // head_groups
    width = group * HD
    norms = n_ref[...].astype(F32)
    _, lane_h, lane_rest = lane_head((rows, LANES))
    for h in range(head_groups):
        out_ref[h, :, :width] = q_ref[:, h * width : (h + 1) * width]
        spread = jnp.zeros((rows, LANES), F32)
        for j in range(group):
            column = norms[:, h * group + j : h * group + j + 1] * (-(HD**0.5))
            spread = jnp.where(lane_h == j, column, spread)
        out_ref[h, :, width : width + LANES] = pick_three(spread, lane_rest)
        at = width + LANES
        out_ref[h, :, at : at + HD] = k_ref[:, h * HD : (h + 1) * HD]
        out_ref[h, :, at + HD : at + 2 * HD] = v_ref[:, h * HD : (h + 1) * HD]
        at += 2 * HD
        out_ref[h, :, at : at + width] = o_ref[:, h * width : (h + 1) * width]


def pack_grads_kernel(place_ref, g_ref, out_ref):
    high_bit, low_bit = place_ref[0], place_ref[1]
    groups, _, wide = out_ref.shape
    width = wide // 4
    for zg in range(groups):
        for rel in range(4):
            block = (
                jnp.bitwise_xor(high_bit, rel // 2) * (2 * groups)
                + 2 * zg
                + jnp.bitwise_xor(low_bit, rel % 2)
            )
            start = pl.multiple_of(block * width, LANES)
            out_ref[zg, :, rel * width : (rel + 1) * width] = g_ref[:, pl.ds(start, width)]


def project_kernel(place_ref, ga, gb, gc, w0, w1, w2, w3, out_ref):
    my_head = place_ref[2]
    groups, rows, wide = ga.shape
    width = wide // 4
    weights = (w0, w1, w2, w3)
    parts = ((ga, 0, 0), (gb, 0, 2), (gc, 0, 1), (gc, groups, 3))
    for ref, at, mask in parts:
        tokens = ref[at : at + groups].reshape(groups * rows, wide)
        total = jnp.zeros((groups * rows, w0.shape[0]), F32)
        for j, w_ref in enumerate(weights):
            total += lax.dot_general(
                tokens[:, j * width : (j + 1) * width],
                w_ref[...],
                (((1,), (1,)), ((), ())),
                preferred_element_type=F32,
            )
        owner = jnp.bitwise_xor(my_head, mask)
        out_ref[:, owner] = total.astype(BF).reshape(groups, rows, -1)


def centre_kernel(p_ref, o_ref, out_ref):
    total = p_ref[0].astype(F32)
    for part in range(1, p_ref.shape[0]):
        total += p_ref[part].astype(F32)
    grads = total.astype(BF)
    rows, width = grads.shape
    out_ref[:, :width] = grads
    product = grads.astype(F32) * o_ref[...].astype(F32)
    _, lane_h, lane_rest = lane_head((rows, LANES))
    spread = jnp.zeros((rows, LANES), F32)
    for j in range(width // HD):
        delta = jnp.sum(product[:, j * HD : (j + 1) * HD], axis=1, keepdims=True)
        spread = jnp.where(lane_h == j, -delta, spread)
    out_ref[:, width:] = pick_three(spread, lane_rest)


def attend_kernel(
    place_ref, qid_ref, kid_ref, q0, q1, q2, q3, d0, d1, d2, d3, kv_ref,
    dq_ref, dkv_ref, q_all, d_all, dq_acc,
):
    step = pl.program_id(0)
    my_inner, my_outer = place_ref[3], place_ref[4]
    part_rows = q0.shape[0]
    rows = 4 * part_rows
    width = q0.shape[1] - LANES
    group = width // HD
    tok = dq_ref.shape[2]

    @pl.when(step == 0)
    def _():
        for part, (q_part, d_part) in enumerate(zip((q0, q1, q2, q3), (d0, d1, d2, d3))):
            at = slice(part * part_rows, (part + 1) * part_rows)
            q_all[at, :width] = q_part[:, :width]
            hidden = jnp.where(kid_ref[...] > qid_ref[at, :], F32(HIDE), F32(0.0))
            q_all[at, width:] = (q_part[:, width:].astype(F32) + hidden).astype(BF)
            d_all[at, :] = d_part[...]
        dq_acc[...] = jnp.zeros_like(dq_acc)

    chunk = kv_ref.shape[0] * kv_ref.shape[1]
    kv = kv_ref[...].reshape(chunk, 2 * HD)
    keys, values = kv[:, :HD], kv[:, HD:]
    lane = lax.broadcasted_iota(jnp.int32, (chunk, LANES), 1)
    block = step * (chunk // tok) + lax.broadcasted_iota(jnp.int32, (chunk, LANES), 0) // tok
    one_hot = jnp.where(lane == ID_LANE + block, F32(1.0), F32(0.0))
    per_step = kv_ref.shape[0]
    diagonal = my_inner // per_step == step

    def run(masked):
        dk = jnp.zeros((chunk, HD), F32)
        dv = jnp.zeros((chunk, HD), F32)
        if masked:
            r = lax.broadcasted_iota(jnp.int32, (chunk, rows), 0)
            c = lax.broadcasted_iota(jnp.int32, (chunk, rows), 1)
            shift = (my_inner % per_step) * (part_rows // tok)
            future = (r // tok - shift == c // tok) & (r % tok > c % tok) & (c < part_rows)
        for j in range(group):
            mine = (lane >= 3 * j) & (lane < 3 * j + 3)
            pick = jnp.where(mine, F32(1.0), F32(0.0))
            keys_wide = jnp.concatenate([keys, (pick + one_hot).astype(BF)], axis=1)
            values_wide = jnp.concatenate([values, pick.astype(BF)], axis=1)
            at = slice(j * HD, (j + 1) * HD)
            q_j, d_j = q_all[:, at], d_all[:, at]
            q_wide = jnp.concatenate([q_j, q_all[:, width:]], axis=1)
            d_wide = jnp.concatenate([d_j, d_all[:, width:]], axis=1)
            contract = (((1,), (1,)), ((), ()))
            scores = lax.dot_general(keys_wide, q_wide, contract, preferred_element_type=F32)
            grad_probs = lax.dot_general(values_wide, d_wide, contract, preferred_element_type=F32)
            probs = jnp.exp2(scores * F32(SCALE * LOG2E))
            if masked:
                probs = jnp.where(future, F32(0.0), probs)
            grad_scores = (probs * grad_probs).astype(BF)
            dv += jnp.dot(probs.astype(BF), d_j, preferred_element_type=F32)
            dk += jnp.dot(grad_scores, q_j, preferred_element_type=F32)
            dq_acc[at, :] += lax.dot_general(
                keys, grad_scores, (((0,), (0,)), ((), ())), preferred_element_type=F32
            )
        dk = (dk * F32(SCALE)).astype(BF)
        dv = dv.astype(BF)
        heads = part_rows // tok
        for i in range(per_step):
            for h in range(heads):
                at = slice((i * heads + h) * tok, (i * heads + h + 1) * tok)
                dkv_ref[h, i, :, :HD] = dk[at]
                dkv_ref[h, i, :, HD:] = dv[at]

    pl.when(diagonal)(lambda: run(True))
    pl.when(jnp.logical_not(diagonal))(lambda: run(False))

    @pl.when(step == pl.num_programs(0) - 1)
    def _():
        for j in range(group):
            at = slice(j * HD, (j + 1) * HD)
            grads = (dq_acc[at, :].T * F32(SCALE)).astype(BF)
            for part in range(4):
                owner = lax.rem(my_outer + 4 - part, 4)
                for h in range(part_rows // tok):
                    start = part * part_rows + h * tok
                    dq_ref[h, owner, :, at] = grads[start : start + tok]


def finish_kernel(dq_ref, dkv_ref, gq_ref, gk_ref, gv_ref):
    heads, parts, _, width = dq_ref.shape
    for h in range(heads):
        total = dq_ref[h, 0].astype(F32)
        for p in range(1, parts):
            total += dq_ref[h, p].astype(F32)
        gq_ref[:, h * width : (h + 1) * width] = total.astype(BF)
        total = dkv_ref[h, 0].astype(F32)
        for p in range(1, dkv_ref.shape[1]):
            total += dkv_ref[h, p].astype(F32)
        total = total.astype(BF)
        gk_ref[:, h * HD : (h + 1) * HD] = total[:, :HD]
        gv_ref[:, h * HD : (h + 1) * HD] = total[:, HD:]


def shape_of(*dims, dtype=BF):
    return jax.ShapeDtypeStruct(dims, dtype)


def body(queries, keys, values, outputs, log_norms, grad_output, w_output, block_order):
    tok = grad_output.shape[0]
    heads = lax.axis_size("head")
    inners = lax.axis_size("inner")
    outers = lax.axis_size("outer")
    head, inner, outer = (lax.axis_index(a) for a in ("head", "inner", "outer"))
    z_count = inners // 2
    z_groups = z_count // 2
    width = queries.shape[1] // heads
    k_width = w_output.shape[1]
    part_rows = heads * tok
    place = jnp.stack([inner // z_count, inner % 2, head, inner, outer]).astype(jnp.int32)
    smem = pl.BlockSpec(memory_space=pltpu.SMEM)
    vmem = pl.BlockSpec(memory_space=pltpu.VMEM)

    weights = [w_output] + [
        lax.ppermute(w_output, "inner", xor_route("inner", m))
        for m in (1, z_count, z_count + 1)
    ]
    grads_out = call(
        pack_grads_kernel,
        shape_of(z_groups, tok, 4 * k_width),
        in_specs=[smem, vmem],
        out_specs=vmem,
    )(place, grad_output)
    strides = [
        [y * z_count + p + 2 * g for g in range(z_groups)] for y in range(2) for p in range(2)
    ]
    grads_a = lax.all_to_all(
        grads_out, "inner", split_axis=0, concat_axis=0, axis_index_groups=strides, tiled=True
    )

    packed = call(
        pack_tokens_kernel,
        shape_of(heads, tok, 2 * width + LANES + 2 * HD),
        in_specs=[vmem] * 5,
        out_specs=vmem,
    )(queries, outputs, keys, values, log_norms)
    mine = lax.all_to_all(packed, "head", split_axis=0, concat_axis=0, tiled=True)
    mine = mine.reshape(part_rows, -1)
    q_part = mine[:, : width + LANES]
    kv_part = mine[:, width + LANES : width + LANES + 2 * HD]
    o_part = mine[:, width + LANES + 2 * HD :]

    grads_b = lax.ppermute(grads_a, "head", xor_route("head", 2))
    grads_c = lax.ppermute(
        jnp.concatenate([grads_a, grads_b], 0), "head", xor_route("head", 1)
    )
    partial = call(
        project_kernel,
        shape_of(z_groups, heads, tok, width),
        in_specs=[smem] + [vmem] * 7,
        out_specs=vmem,
    )(place, grads_a, grads_b, grads_c, *weights)
    partial = lax.all_to_all(
        partial, "inner", split_axis=0, concat_axis=0, axis_index_groups=strides, tiled=True
    )
    d_part = call(
        centre_kernel,
        shape_of(part_rows, width + LANES),
        in_specs=[vmem] * 2,
        out_specs=vmem,
    )(partial.reshape(z_groups, part_rows, width), o_part)

    def around(x):
        return [x] + [
            lax.ppermute(x, "outer", [(i, (i + d) % outers) for i in range(outers)])
            for d in range(1, outers)
        ]

    q_parts = around(q_part)
    kv_all = lax.all_to_all(
        jnp.broadcast_to(kv_part[None], (inners,) + kv_part.shape),
        "inner", split_axis=0, concat_axis=0, tiled=True,
    )
    d_parts = around(d_part)

    order = block_order.reshape(heads, inners, outers)
    k_ids = lax.dynamic_index_in_dim(order, outer, 2, keepdims=False).T.reshape(-1)
    q_ids = lax.dynamic_index_in_dim(order, inner, 1, keepdims=False).T
    q_ids = jnp.concatenate(
        [lax.dynamic_index_in_dim(q_ids, (outer - d) % outers, 0) for d in range(outers)], 0
    ).reshape(-1)
    kid_row = jnp.full((1, LANES), -1.0, F32)
    kid_row = lax.dynamic_update_slice(kid_row, k_ids.astype(F32)[None], (0, ID_LANE))
    qid_col = jnp.repeat(q_ids.astype(F32), tok)[:, None]

    per_step = CHUNK // part_rows
    rows = outers * part_rows
    whole = lambda *shape: pl.BlockSpec(shape, lambda c: (0,) * len(shape))
    dq_out, dkv_out = call(
        attend_kernel,
        (
            shape_of(heads, outers, tok, width),
            shape_of(heads, inners, tok, 2 * HD),
        ),
        grid=(inners // per_step,),
        in_specs=[smem, whole(rows, 1), whole(1, LANES)]
        + [whole(part_rows, width + LANES)] * 8
        + [pl.BlockSpec((per_step, part_rows, 2 * HD), lambda c: (c, 0, 0))],
        out_specs=(
            whole(heads, outers, tok, width),
            pl.BlockSpec((heads, per_step, tok, 2 * HD), lambda c: (0, c, 0, 0)),
        ),
        scratch_shapes=[
            pltpu.VMEM((rows, width + LANES), BF),
            pltpu.VMEM((rows, width + LANES), BF),
            pltpu.VMEM((width, rows), F32),
        ],
    )(place, qid_col, kid_row, *q_parts, *d_parts, kv_all)

    dq_back = lax.all_to_all(
        dq_out.reshape(heads * outers, tok, width),
        ("head", "outer"), split_axis=0, concat_axis=0, tiled=True,
    ).reshape(heads, outers, tok, width)
    dkv_back = lax.all_to_all(
        dkv_out.reshape(heads * inners, tok, 2 * HD),
        ("head", "inner"), split_axis=0, concat_axis=0, tiled=True,
    ).reshape(heads, inners, tok, 2 * HD)
    return call(
        finish_kernel,
        (
            shape_of(tok, heads * width),
            shape_of(tok, heads * HD),
            shape_of(tok, heads * HD),
        ),
        in_specs=[vmem] * 2,
        out_specs=(vmem,) * 3,
    )(dq_back, dkv_back)


def solution(mesh):
    tokens = P(("head", "inner", "outer"), None)
    in_specs = (tokens,) * 6 + (P("head", "inner"), P())
    return jax.shard_map(
        body, mesh=mesh, in_specs=in_specs, out_specs=(tokens,) * 3, check_vma=False
    )
```

time: 1150 us -> 209 us (0.18)
  waiting for transfers between devices: 742 us -> 55.7 us
  starting transfers between devices: 168 us -> 33.8 us
  blocking collectives: 0 us -> 77.1 us
  matrix products: 76.8 us -> 0 us
  local copies, waits for them, and re-layouts: 77.6 us -> 10 us
  other arithmetic: 65.2 us -> 1.13 us
  Pallas kernels: 0 us -> 29.5 us
  between operations: 13.8 us -> 0.77 us
    reduce_scatter x1 -> x0, waiting for transfers between devices: 324 us -> none  [body(): lax.psum_scatter(grad_state, ('inner', 'outer'), scatter_dimension=0, til...]
    ppermute x134 -> x11, waiting for transfers between devices: 247 us -> 26.7 us  [the longest x3 17.1 us: body(): lax.ppermute(w_output, 'inner', xor_route('inner', m))]
    all_gather x2 -> x0, waiting for transfers between devices: 152 us -> none  [the longest x1 152 us: body(): lax.all_gather(w_output, 'inner', axis=1, tiled=True)]
    all_to_all x8 -> x3, starting transfers between devices: 158 us -> 17.3 us  [the longest x1 8.88 us: body(): lax.all_to_all(jnp.broadcast_to(kv_part[None], (inners,) + kv_part.shape)...]
    all_to_all x0 -> x3, blocking collectives: none -> 77.1 us  [the longest x1 36.6 us: body(): lax.all_to_all(dkv_out.reshape(heads * inners, tok, 2 * HD), ('head', 'in...]
    dot_general x321 -> x0, matrix products: 76.8 us -> none  [the longest x64 16.8 us: tile_terms(): jnp.einsum('qgjd,kgd->gjqk', query_four, key_three, preferred_element_typ...]
    dynamic_update_slice x64 -> x0, other arithmetic: 44 us -> none  [inner_step(): lax.dynamic_update_slice_in_dim(state_cur, jnp.concatenate([part_k, part_...]
    gather x65 -> x0, local copies, waits for them, and re-layouts: 42.3 us -> none  [positions(): block_order[jnp.arange(sub_count, dtype=jnp.int32) * ctx_count + owner_rank]]
  transfers between devices with their start and end apart: 145 -> 14, of which waited for: 141 -> 9; matrix products, arithmetic and copies ran while one was open for 18% -> 2% of each run, Pallas kernels for 0% -> 3%
where the time goes in v1:
time: 209 us; the launch traced here: 208 us
  blocking collectives  77.1 us (37%)
  waiting for transfers between devices  55.7 us (27%)
  starting transfers between devices  33.8 us (16%)
  Pallas kernels  29.5 us (14%)
  local copies, waits for them, and re-layouts  10 us (5%)
    all_to_all x1, blocking collectives, body(): lax.all_to_all(dkv_out.reshape(heads * inners, tok, 2 * HD), ('head', 'in...  36.6 us
    pallas_call x1, Pallas kernels, body(): call(attend_kernel, (shape_of(heads, outers, tok, width), shape_of(heads,...  21.9 us
    all_to_all x1, blocking collectives, body(): lax.all_to_all(grads_out, 'inner', split_axis=0, concat_axis=0, axis_inde...  20.9 us
    all_to_all x1, blocking collectives, body(): lax.all_to_all(dq_out.reshape(heads * outers, tok, width), ('head', 'oute...  19.6 us
    ppermute x3, waiting for transfers between devices, body(): lax.ppermute(w_output, 'inner', xor_route('inner', m))  17.1 us
    all_to_all x1, waiting for transfers between devices, body(): lax.all_to_all(partial, 'inner', split_axis=0, concat_axis=0, axis_index_...  16.8 us
    all_to_all x1, waiting for transfers between devices, body(): lax.all_to_all(jnp.broadcast_to(kv_part[None], (inners,) + kv_part.shape)...  11.9 us
    all_to_all x1, starting transfers between devices, body(): lax.all_to_all(jnp.broadcast_to(kv_part[None], (inners,) + kv_part.shape)...  8.88 us
  transfers between devices with their start and end apart: 14, of which 9 were waited for; matrix products, arithmetic and copies ran while one was open for 2% of the time, Pallas kernels for 3%

profile of v1, /device:TPU:1, one launch (start us, length us, event | category | flops | bytes accessed | tf_op | source)
XLA Modules:
  0.0 208.1 jit_solution(18121400910068363703)
XLA Ops:
  0.7 1.0 copy-done.1
  1.7 0.6 shard_map.104
  2.3 20.9 %all_to_all.30.ga = bf16[4,32,1536]{2,1,0:T(8,128)(2,1)S(1)} all-to-all(bf16[4,32,1536]{2,1,0:T(8,128)(2,1)S(1)} %shard_map.104), channel_id=1, replica_groups={{0,8,16,24},{4,12,20,28},{32,40,48,56},{36,44,52,60},{1,9,17,25},{5,13,..., dimensions={0} | all-to-all | bytes 786432 | tf_op jit(solution)/shard_map/all_to_all | solution.py:259
  23.3 1.3 collective-permute-start.3
  24.6 6.6 %collective-permute-done.3.gb = bf16[4,32,1536]{2,1,0:T(8,128)(2,1)S(1)} collective-permute-done((bf16[4,32,1536]{2,1,0:T(8,128)(2,1)S(1)}, bf16[4,32,1536]{2,1,0:T(8,128)(2,1)S(1)}, u32[]{:S(2)}, u32[]{:S(2)}) %collective-permute-start.3) | collective-permute-done | bytes 393248 | tf_op jit(solution)/shard_map/ppermute | solution.py:275
  31.2 1.0 pad_maximum_fusion
  32.2 3.6 %collective-permute-start.4 = (bf16[8,32,1536]{2,1,0:T(8,128)(2,1)}, bf16[8,32,1536]{2,1,0:T(8,128)(2,1)S(1)}, u32[]{:S(2)}, u32[]{:S(2)}) collective-permute-start(bf16[8,32,1536]{2,1,0:T(8,128)(2,1)} %pad_maximum_fusion), channel_id=1, source_target_pairs={{0,64},{64,0},{128,192},{192,128},{1,65},{65,1},{129,193},{193,129... | collective-permute-start | bytes 2359304 | tf_op jit(solution)/shard_map/ppermute | solution.py:276
  35.8 1.0 collective-permute-start.5
  36.8 2.9 %collective-permute-start.6 = (bf16[768,384]{1,0:T(8,128)(2,1)S(1)}, bf16[768,384]{1,0:T(8,128)(2,1)S(1)}, u32[]{:S(2)}, u32[]{:S(2)}) collective-permute-start(bf16[768,384]{1,0:T(8,128)(2,1)S(1)} %copy-done), channel_id=1, source_target_pairs={{0,32},{4,36},{8,40},{12,44},{16,48},{20,52},{24,56},{28,60},{32,0... | collective-permute-start | bytes 1769480 | tf_op jit(solution)/shard_map/ppermute | solution.py:247
  39.7 0.2 collective-permute-start.7
  39.9 0.8 copy.17.n_ref
  40.7 0.9 copy-done.3
  41.6 0.8 copy-done.4
  42.4 0.8 copy-done.5
  43.1 1.0 shard_map.103
  44.1 4.9 %all-to-all-start = ((bf16[4,32,1920]{2,1,0:T(8,128)(2,1)}), bf16[4,32,1920]{2,1,0:T(8,128)(2,1)}, u32[]{:S(2)}, u32[]{:S(2)}) async-start(bf16[4,32,1920]{2,1,0:T(8,128)(2,1)} %shard_map.103), calls=%async_computation | async-start | bytes 983040 | tf_op jit(solution)/shard_map/all_to_all | solution.py:269
  49.1 1.7 collective-permute-done.5.w1
  50.7 14.1 %collective-permute-done.6.w2 = bf16[768,384]{1,0:T(8,128)(2,1)S(1)} collective-permute-done((bf16[768,384]{1,0:T(8,128)(2,1)S(1)}, bf16[768,384]{1,0:T(8,128)(2,1)S(1)}, u32[]{:S(2)}, u32[]{:S(2)}) %collective-permute-start.6) | collective-permute-done | bytes 589856 | tf_op jit(solution)/shard_map/ppermute | solution.py:247
  64.8 1.4 collective-permute-done.7.w3
  66.1 4.9 %shard_map.105 = bf16[4,4,32,768]{3,2,1,0:T(8,128)(2,1)} custom-call(s32[5]{0:T(128)S(1)} %stack.23.place_ref, bf16[4,32,1536]{2,1,0:T(8,128)(2,1)S(1)} %all_to_all.30.ga, bf16[4,32,1536]{2,1,0:T(8,128)(2,1)S(1)} %collective-permute-done.3.gb, bf16[8,32,1536]{2,1,0:T(8,128)(2,1)S(1)} %collective-permute-done.4.gc, bf16[768,384]{1,0:T(8,128)(2,1)S(1)} %copy-done, ...), custom_call_target="tpu_custom_call" | custom-call | tf_op jit(solution)/shard_map/pallas_call | solution.py:279
  71.0 0.3 all-to-all-done
  71.3 3.5 %all-to-all-start.2 = ((bf16[4,4,32,768]{3,2,1,0:T(8,128)(2,1)}), bf16[4,4,32,768]{3,2,1,0:T(8,128)(2,1)S(1)}, u32[]{:S(2)}, u32[]{:S(2)}) async-start(bf16[4,4,32,768]{3,2,1,0:T(8,128)(2,1)} %shard_map.105), calls=%async_computation.2 | async-start | bytes 1572864 | tf_op jit(solution)/shard_map/all_to_all | solution.py:285
  74.8 0.8 slice.14
  75.6 16.8 %all-to-all-done.2 = bf16[4,4,32,768]{3,2,1,0:T(8,128)(2,1)S(1)} async-done(((bf16[4,4,32,768]{3,2,1,0:T(8,128)(2,1)}), bf16[4,4,32,768]{3,2,1,0:T(8,128)(2,1)S(1)}, u32[]{:S(2)}, u32[]{:S(2)}) %all-to-all-start.2) | async-done | bytes 786464 | tf_op jit(solution)/shard_map/all_to_all | solution.py:285
  92.5 1.1 broadcast_in_dim.5
  93.5 8.9 %all-to-all-start.3 = ((bf16[16,128,256]{2,1,0:T(8,128)(2,1)}), bf16[16,128,256]{2,1,0:T(8,128)(2,1)S(1)}, u32[]{:S(2)}, u32[]{:S(2)}) async-start(bf16[16,128,256]{2,1,0:T(8,128)(2,1)} %broadcast_in_dim.5), calls=%async_computation.3 | async-start | bytes 2097152 | tf_op jit(solution)/shard_map/all_to_all | solution.py:302
  102.4 1.0 slice.12.q0
  103.4 1.3 collective-permute-start
  104.7 0.9 slice.13.o_ref
  105.6 2.5 %collective-permute-start.1 = (bf16[128,896]{1,0:T(8,128)(2,1)S(1)}, bf16[128,896]{1,0:T(8,128)(2,1)S(1)}, u32[]{:S(2)}, u32[]{:S(2)}) collective-permute-start(bf16[128,896]{1,0:T(8,128)(2,1)S(1)} %slice.12.q0), channel_id=1, source_target_pairs={{0,2},{1,3},{2,0},{3,1},{4,6},{5,7},{6,4},{7,5},{8,10},{9,11},{10,... | collective-permute-start | bytes 688136 | tf_op jit(solution)/shard_map/ppermute | solution.py:297
  108.2 1.1 collective-permute-start.2
  109.3 0.2 shard_map.106.d0
  109.6 1.5 collective-permute-start.8
  111.1 1.0 collective-permute-start.9
  112.1 0.7 copy-done.6
  112.8 0.1 reshape.55
  112.9 0.5 dynamic-slice_reduce_fusion.3
  113.5 0.3 broadcast_in_dim_reshape.4.qid_ref
  113.8 0.2 convert_reduce_fusion
  114.0 0.1 copy.16
  114.0 0.1 convert_element_type.30
  114.2 2.3 %collective-permute-done.1.q2 = bf16[128,896]{1,0:T(8,128)(2,1)S(1)} collective-permute-done((bf16[128,896]{1,0:T(8,128)(2,1)S(1)}, bf16[128,896]{1,0:T(8,128)(2,1)S(1)}, u32[]{:S(2)}, u32[]{:S(2)}) %collective-permute-start.1) | collective-permute-done | bytes 229408 | tf_op jit(solution)/shard_map/ppermute | solution.py:297
  116.5 0.6 collective-permute-done.2.q3
  117.2 11.9 %all-to-all-done.3.kv_ref = bf16[16,128,256]{2,1,0:T(8,128)(2,1)S(1)} async-done(((bf16[16,128,256]{2,1,0:T(8,128)(2,1)}), bf16[16,128,256]{2,1,0:T(8,128)(2,1)S(1)}, u32[]{:S(2)}, u32[]{:S(2)}) %all-to-all-start.3) | async-done | bytes 1048608 | tf_op jit(solution)/shard_map/all_to_all | solution.py:302
  129.0 21.9 %shard_map.107 = (bf16[4,4,32,768]{3,2,1,0:T(8,128)(2,1)S(1)}, bf16[4,16,32,256]{3,2,1,0:T(8,128)(2,1)S(1)}) custom-call(s32[5]{0:T(128)S(1)} %stack.23.place_ref, f32[512,1]{1,0:T(8,128)S(1)} %broadcast_in_dim_reshape.4.qid_ref, f32[1,128]{1,0:T(1,128)S(1)} %dynamic_update_slice.3.kid_ref, bf16[128,896]{1,0:T(8,128)(2,1)S(1)} %slice.12.q0, ...), custom_call_target="tpu_custom_call" | custom-call | tf_op jit(solution)/shard_map/pallas_call | solution.py:321
  151.0 19.6 %all_to_all.31 = bf16[16,32,768]{2,1,0:T(8,128)(2,1)S(1)} all-to-all(bf16[16,32,768]{2,1,0:T(8,128)(2,1)S(1)} %bitcast.20), channel_id=1, replica_groups=mesh['head'=4,'inner'=16,'outer'=4] {'head','outer'}, dimensions={0} | all-to-all | bytes 1572864 | tf_op jit(solution)/shard_map/all_to_all | solution.py:342
  170.6 36.6 %all_to_all.32 = bf16[64,32,256]{2,1,0:T(8,128)(2,1)S(1)} all-to-all(bf16[64,32,256]{2,1,0:T(8,128)(2,1)S(1)} %bitcast.19), channel_id=1, replica_groups=mesh['head'=4,'inner'=16,'outer'=4] {'head','inner'}, dimensions={0} | all-to-all | bytes 2097152 | tf_op jit(solution)/shard_map/all_to_all | solution.py:346
  207.2 0.9 shard_map.108
  (20 shorter events, 0.4 us)
Async XLA Ops:
  0.7 1.0 copy-start.1
  23.3 12.5 %copy-start = (bf16[768,384]{1,0:T(8,128)(2,1)S(1)}, bf16[768,384]{1,0:T(8,128)(2,1)}, u32[]{:S(2)}) copy-start(bf16[768,384]{1,0:T(8,128)(2,1)} %w0.1) | copy-start | bytes 1769476
  23.3 17.4 %copy-start.2 = (bf16[32,3072]{1,0:T(8,128)(2,1)S(1)}, bf16[32,3072]{1,0:T(8,128)(2,1)}, u32[]{:S(2)}) copy-start(bf16[32,3072]{1,0:T(8,128)(2,1)} %q_ref.1) | copy-start | bytes 589828
  23.3 7.9 %collective-permute-start.3 = (bf16[4,32,1536]{2,1,0:T(8,128)(2,1)S(1)}, bf16[4,32,1536]{2,1,0:T(8,128)(2,1)S(1)}, u32[]{:S(2)}, u32[]{:S(2)}) collective-permute-start(bf16[4,32,1536]{2,1,0:T(8,128)(2,1)S(1)} %all_to_all.30.ga), channel_id=1, source_target_pairs={{0,128},{64,192},{128,0},{192,64},{1,129},{65,193},{129,1},{193,65... | collective-permute-start | bytes 1179656 | tf_op jit(solution)/shard_map/ppermute | solution.py:275
  32.2 34.0 %collective-permute-start.4 = (bf16[8,32,1536]{2,1,0:T(8,128)(2,1)}, bf16[8,32,1536]{2,1,0:T(8,128)(2,1)S(1)}, u32[]{:S(2)}, u32[]{:S(2)}) collective-permute-start(bf16[8,32,1536]{2,1,0:T(8,128)(2,1)} %pad_maximum_fusion), channel_id=1, source_target_pairs={{0,64},{64,0},{128,192},{192,128},{1,65},{65,1},{129,193},{193,129... | collective-permute-start | bytes 2359304 | tf_op jit(solution)/shard_map/ppermute | solution.py:276
  35.8 15.0 %collective-permute-start.5 = (bf16[768,384]{1,0:T(8,128)(2,1)S(1)}, bf16[768,384]{1,0:T(8,128)(2,1)S(1)}, u32[]{:S(2)}, u32[]{:S(2)}) collective-permute-start(bf16[768,384]{1,0:T(8,128)(2,1)S(1)} %copy-done), channel_id=1, source_target_pairs={{0,4},{4,0},{8,12},{12,8},{16,20},{20,16},{24,28},{28,24},{32,36},... | collective-permute-start | bytes 1769480 | tf_op jit(solution)/shard_map/ppermute | solution.py:247
  36.8 28.0 %collective-permute-start.6 = (bf16[768,384]{1,0:T(8,128)(2,1)S(1)}, bf16[768,384]{1,0:T(8,128)(2,1)S(1)}, u32[]{:S(2)}, u32[]{:S(2)}) collective-permute-start(bf16[768,384]{1,0:T(8,128)(2,1)S(1)} %copy-done), channel_id=1, source_target_pairs={{0,32},{4,36},{8,40},{12,44},{16,48},{20,52},{24,56},{28,60},{32,0... | collective-permute-start | bytes 1769480 | tf_op jit(solution)/shard_map/ppermute | solution.py:247
  39.7 26.4 %collective-permute-start.7 = (bf16[768,384]{1,0:T(8,128)(2,1)S(1)}, bf16[768,384]{1,0:T(8,128)(2,1)}, u32[]{:S(2)}, u32[]{:S(2)}) collective-permute-start(bf16[768,384]{1,0:T(8,128)(2,1)S(1)} %copy-done), channel_id=1, source_target_pairs={{0,36},{4,32},{8,44},{12,40},{16,52},{20,48},{24,60},{28,56},{32,4... | collective-permute-start | bytes 1769480 | tf_op jit(solution)/shard_map/ppermute | solution.py:247
  40.7 0.9 copy-start.3
  41.6 0.8 copy-start.4
  42.4 0.8 copy-start.5
  44.1 27.2 %all-to-all-start = ((bf16[4,32,1920]{2,1,0:T(8,128)(2,1)}), bf16[4,32,1920]{2,1,0:T(8,128)(2,1)}, u32[]{:S(2)}, u32[]{:S(2)}) async-start(bf16[4,32,1920]{2,1,0:T(8,128)(2,1)} %shard_map.103), calls=%async_computation | async-start | bytes 983040 | tf_op jit(solution)/shard_map/all_to_all | solution.py:269
  71.3 21.2 %all-to-all-start.2 = ((bf16[4,4,32,768]{3,2,1,0:T(8,128)(2,1)}), bf16[4,4,32,768]{3,2,1,0:T(8,128)(2,1)S(1)}, u32[]{:S(2)}, u32[]{:S(2)}) async-start(bf16[4,4,32,768]{3,2,1,0:T(8,128)(2,1)} %shard_map.105), calls=%async_computation.2 | async-start | bytes 1572864 | tf_op jit(solution)/shard_map/all_to_all | solution.py:285
  93.5 35.5 %all-to-all-start.3 = ((bf16[16,128,256]{2,1,0:T(8,128)(2,1)}), bf16[16,128,256]{2,1,0:T(8,128)(2,1)S(1)}, u32[]{:S(2)}, u32[]{:S(2)}) async-start(bf16[16,128,256]{2,1,0:T(8,128)(2,1)} %broadcast_in_dim.5), calls=%async_computation.3 | async-start | bytes 2097152 | tf_op jit(solution)/shard_map/all_to_all | solution.py:302
  103.4 7.7 %collective-permute-start = (bf16[128,896]{1,0:T(8,128)(2,1)S(1)}, bf16[128,896]{1,0:T(8,128)(2,1)S(1)}, u32[]{:S(2)}, u32[]{:S(2)}) collective-permute-start(bf16[128,896]{1,0:T(8,128)(2,1)S(1)} %slice.12.q0), channel_id=1, source_target_pairs={{0,1},{1,2},{2,3},{3,0},{4,5},{5,6},{6,7},{7,4},{8,9},{9,10},{10,1... | collective-permute-start | bytes 688136 | tf_op jit(solution)/shard_map/ppermute | solution.py:297
  105.6 10.9 %collective-permute-start.1 = (bf16[128,896]{1,0:T(8,128)(2,1)S(1)}, bf16[128,896]{1,0:T(8,128)(2,1)S(1)}, u32[]{:S(2)}, u32[]{:S(2)}) collective-permute-start(bf16[128,896]{1,0:T(8,128)(2,1)S(1)} %slice.12.q0), channel_id=1, source_target_pairs={{0,2},{1,3},{2,0},{3,1},{4,6},{5,7},{6,4},{7,5},{8,10},{9,11},{10,... | collective-permute-start | bytes 688136 | tf_op jit(solution)/shard_map/ppermute | solution.py:297
  108.2 9.0 %collective-permute-start.2 = (bf16[128,896]{1,0:T(8,128)(2,1)S(1)}, bf16[128,896]{1,0:T(8,128)(2,1)S(1)}, u32[]{:S(2)}, u32[]{:S(2)}) collective-permute-start(bf16[128,896]{1,0:T(8,128)(2,1)S(1)} %slice.12.q0), channel_id=1, source_target_pairs={{0,3},{1,0},{2,1},{3,2},{4,7},{5,4},{6,5},{7,6},{8,11},{9,8},{10,9... | collective-permute-start | bytes 688136 | tf_op jit(solution)/shard_map/ppermute | solution.py:297
  109.6 19.5 %collective-permute-start.10 = (bf16[128,896]{1,0:T(8,128)(2,1)S(1)}, bf16[128,896]{1,0:T(8,128)(2,1)S(1)}, u32[]{:S(2)}, u32[]{:S(2)}) collective-permute-start(bf16[128,896]{1,0:T(8,128)(2,1)S(1)} %shard_map.106.d0), channel_id=1, source_target_pairs={{0,3},{1,0},{2,1},{3,2},{4,7},{5,4},{6,5},{7,6},{8,11},{9,8},{10,9... | collective-permute-start | bytes 688136 | tf_op jit(solution)/shard_map/ppermute | solution.py:297
  109.6 19.4 %collective-permute-start.8 = (bf16[128,896]{1,0:T(8,128)(2,1)S(1)}, bf16[128,896]{1,0:T(8,128)(2,1)S(1)}, u32[]{:S(2)}, u32[]{:S(2)}) collective-permute-start(bf16[128,896]{1,0:T(8,128)(2,1)S(1)} %shard_map.106.d0), channel_id=1, source_target_pairs={{0,1},{1,2},{2,3},{3,0},{4,5},{5,6},{6,7},{7,4},{8,9},{9,10},{10,1... | collective-permute-start | bytes 688136 | tf_op jit(solution)/shard_map/ppermute | solution.py:297
  111.1 17.9 %collective-permute-start.9 = (bf16[128,896]{1,0:T(8,128)(2,1)S(1)}, bf16[128,896]{1,0:T(8,128)(2,1)S(1)}, u32[]{:S(2)}, u32[]{:S(2)}) collective-permute-start(bf16[128,896]{1,0:T(8,128)(2,1)S(1)} %shard_map.106.d0), channel_id=1, source_target_pairs={{0,2},{1,3},{2,0},{3,1},{4,6},{5,7},{6,4},{7,5},{8,10},{9,11},{10,... | collective-permute-start | bytes 688136 | tf_op jit(solution)/shard_map/ppermute | solution.py:297
  112.1 0.7 copy-start.6
